TPU v7x, 768 devices: a whole 4x8x12 slice. The times are simulated.
768 devices in a mesh: dom: 16 (over y, core), grp: 48 (over z, x).
Axes of the slice: x: 4, y: 8, z: 12, core: 2. Of those that a mesh axis runs over, the one named last changes fastest.
Arguments:
- features: bfloat16 [196608, 256], P(('dom', 'grp')), may hold values from -6 to 6
- w_self: bfloat16 [256, 256], replicated, may hold values from -0.375 to 0.375
- w_neigh: bfloat16 [256, 256], replicated, may hold values from -9 to 9
- adjacency: bfloat16 [1536, 8, 128, 128], P(('dom', 'grp')), may hold values from 0 to 1
- tile_ids: int32 [1536, 8], P(('dom', 'grp')), may hold values from 0 to 11
- send_rows: int32 [12288, 32], P(('dom', 'grp')), may hold values from 0 to 255
- send_counts: int32 [768, 16], P(('dom', 'grp')), may hold values from 1 to 32, 256 in all within a row
- hub_rows: int32 [768, 16], P(('dom', 'grp')), may hold values from 0 to 255
- cotangent: bfloat16 [196608, 256], P(('dom', 'grp')), may hold values from -6 to 6
Outputs:
- output: bfloat16 [196608, 256], P(('dom', 'grp'))
- grad_features: bfloat16 [196608, 256], P(('dom', 'grp'))
- grad_self: float32 [256, 256], replicated
- grad_neigh: float32 [256, 256], replicated
Inputs may be any that keep to these rules, and one draw needn't show every extreme that they name: `send_counts`: each device's counts to the 16 partitions sum to 256; on every device one count is exactly 32. `send_rows`: rows may repeat within a list. `hub_rows`: rows may repeat. `tile_ids`: A column tile may be read by several stored tiles or by none.
All inputs are finite; a program needn't handle non-finite values.
Results may differ from a plain program's by a relative error of at most 0.0057.
Values may be sent and summed in bfloat16 or wider, within the bound.
A program may use at most 32 MiB of HBM per device.

v0:
```python
import jax
import jax.numpy as jnp
from jax import lax
from jax.sharding import PartitionSpec as P


def local_layer(own_rows, halo_rows, hub_feats, adjacency, tile_index, w_self, w_neigh, cotangent):
    node_count, feat_width = own_rows.shape
    tile_size = adjacency.shape[2]
    source = jnp.concatenate([own_rows, halo_rows, hub_feats], axis=0)
    src_count = source.shape[0] // tile_size
    src_tiles = source.reshape(src_count, tile_size, feat_width)
    picked = src_tiles[tile_index]
    numer = jnp.einsum("rtij,rtjf->rif", adjacency, picked, preferred_element_type=jnp.float32)
    denom = 1.0 + jnp.sum(adjacency.astype(jnp.float32), axis=(1, 3))
    agg = (numer / denom[..., None]).reshape(node_count, feat_width).astype(jnp.bfloat16)
    preact = jnp.dot(own_rows, w_self, preferred_element_type=jnp.float32) + jnp.dot(
        agg, w_neigh, preferred_element_type=jnp.float32
    )
    sigmoid_pre = jax.nn.sigmoid(preact)
    output = (preact * sigmoid_pre).astype(jnp.bfloat16)
    grad_pre = (
        cotangent.astype(jnp.float32) * sigmoid_pre * (1.0 + preact * (1.0 - sigmoid_pre))
    ).astype(jnp.bfloat16)
    grad_ws = jnp.dot(own_rows.T, grad_pre, preferred_element_type=jnp.float32)
    grad_wn = jnp.dot(agg.T, grad_pre, preferred_element_type=jnp.float32)
    grad_own = jnp.dot(grad_pre, w_self.T, preferred_element_type=jnp.float32)
    grad_agg = jnp.dot(grad_pre, w_neigh.T, preferred_element_type=jnp.float32)
    grad_num = (grad_agg.reshape(numer.shape) / denom[..., None]).astype(jnp.bfloat16)
    contrib = jnp.einsum("rtij,rif->rtjf", adjacency, grad_num, preferred_element_type=jnp.float32)
    grad_source = (
        jnp.zeros((src_count, tile_size, feat_width), jnp.float32)
        .at[tile_index.reshape(-1)]
        .add(contrib.reshape(-1, tile_size, feat_width))
        .reshape(-1, feat_width)
    )
    halo_count = halo_rows.shape[0]
    return (
        output,
        grad_ws,
        grad_wn,
        grad_own + grad_source[:node_count],
        grad_source[node_count : node_count + halo_count],
        grad_source[node_count + halo_count :],
    )


def on_device(
    features, w_self, w_neigh, adjacency, tile_ids, send_rows, send_counts, hub_rows, cotangent
):
    node_count, feat_width = features.shape
    send_slots = send_rows.shape[1]
    live_slots = jnp.arange(send_slots, dtype=jnp.int32)[None, :] < send_counts[0][:, None]
    outgoing = jnp.where(live_slots[..., None], features[send_rows], jnp.zeros((), jnp.bfloat16))
    received = lax.all_to_all(outgoing, "dom", split_axis=0, concat_axis=0, tiled=True)
    halo_rows = received.reshape(-1, feat_width)
    hub_feats = lax.all_gather(features[hub_rows[0]], "grp", axis=0, tiled=True)
    output, grad_ws, grad_wn, grad_own, grad_halo, grad_hub = local_layer(
        features, halo_rows, hub_feats, adjacency, tile_ids, w_self, w_neigh, cotangent
    )
    returned = lax.all_to_all(
        grad_halo.reshape(outgoing.shape).astype(jnp.bfloat16),
        "dom",
        split_axis=0,
        concat_axis=0,
        tiled=True,
    ).astype(jnp.float32)
    returned = jnp.where(live_slots[..., None], returned, jnp.zeros((), jnp.float32))
    grad_rows = grad_own.at[send_rows.reshape(-1)].add(returned.reshape(-1, feat_width))
    hub_total = lax.psum_scatter(grad_hub, "grp", scatter_dimension=0, tiled=True)
    grad_rows = grad_rows.at[hub_rows[0]].add(hub_total)
    grad_self, grad_neigh = lax.psum((grad_ws, grad_wn), ("dom", "grp"))
    return (output, grad_rows.astype(jnp.bfloat16), grad_self, grad_neigh)


def solution(mesh):
    placed = (
        P(("dom", "grp"), None),
        P(),
        P(),
        P(("dom", "grp"), None, None, None),
        P(("dom", "grp"), None),
        P(("dom", "grp"), None),
        P(("dom", "grp"), None),
        P(("dom", "grp"), None),
        P(("dom", "grp"), None),
    )
    return jax.shard_map(
        on_device,
        mesh=mesh,
        in_specs=placed,
        out_specs=(P(("dom", "grp"), None), P(("dom", "grp"), None), P(), P()),
        check_vma=False,
    )
```

profile of v0, /device:TPU:1, one launch (start us, length us, event | category | flops | bytes accessed | tf_op | source)
XLA Modules:
  0.0 591.0 jit_solution(12449768577173497995)
XLA Ops:
  8.0 0.0 copy-start
  8.0 0.8 iota_compare_fusion
  8.8 0.7 compare_select_fusion
  9.5 0.1 reshape.158
  9.6 0.0 copy-start.6
  9.6 0.0 copy-start.8
  9.6 0.0 copy-start.1
  9.6 0.0 copy-start.2
  9.6 2.5 gather_fusion
  12.2 0.0 copy-start.3
  12.2 0.8 broadcast_select_fusion
  13.0 13.8 %all-to-all-start = ((bf16[16,32,256]{2,1,0:T(8,128)(2,1)}), bf16[16,32,256]{2,1,0:T(8,128)(2,1)S(1)}, u32[]{:S(2)}, u32[]{:S(2)}) async-start(bf16[16,32,256]{2,1,0:T(8,128)(2,1)} %broadcast_select_fusion), calls=%async_computation | async-start | bytes 524288 | tf_op jit(solution)/shard_map/all_to_all | solution.py:55
  26.9 0.0 all-reduce.3.cloned.1.call-start
  26.9 0.0 copy-done.6
  26.9 0.1 reshape.151
  27.0 0.0 copy-done.8
  27.0 0.0 copy-done.1
  27.0 0.6 gather_fusion.1
  27.6 0.1 reshape.174
  27.7 0.0 copy-done.2
  27.7 0.1 convert_reduce_fusion
  27.9 60.2 %all-gather = bf16[768,256]{1,0:T(8,128)(2,1)S(1)} all-gather(bf16[16,256]{1,0:T(8,128)(2,1)S(1)} %gather_fusion.1), channel_id=2, replica_groups=mesh['dom'=16,'grp'=48] {'grp'}, dimensions={0}, use_global_device_ids=true | all-gather | bytes 401408 | tf_op jit(solution)/shard_map/all_gather | solution.py:57
  88.1 0.0 copy-done.3
  88.1 0.2 fusion.6
  88.3 0.0 all-to-all-done
  88.3 0.1 pad_maximum_fusion
  88.3 0.6 gather_fusion.2
  89.0 0.0 copy-start.7
  89.0 0.3 fusion.1
  89.3 0.0 copy-done
  89.3 0.6 copy-done.7
  89.9 0.9 multiply_convert_fusion
  90.8 0.2 fusion.7
  91.0 0.9 fusion.8
  92.0 0.9 convolution_bitcast_fusion
  92.9 0.1 copy.13
  93.0 0.0 all-reduce.3.cloned.1.call-update
  93.0 0.0 reduce-scatter.2.cloned.1.call-start
  93.1 0.4 fusion.2
  93.5 1.9 copy.14
  95.4 0.1 broadcast_in_dim.44
  95.5 3.5 scatter_fusion
  99.0 0.0 copy-start.5
  99.0 0.9 slice.30
  100.0 0.0 reduce-scatter.2.cloned.1.call-update
  100.0 0.7 slice.32
  100.7 25.9 %all-to-all-start.1 = ((bf16[16,32,256]{2,1,0:T(8,128)(2,1)}), bf16[16,32,256]{2,1,0:T(8,128)(2,1)S(1)}, u32[]{:S(2)}, u32[]{:S(2)}) async-start(bf16[16,32,256]{2,1,0:T(8,128)(2,1)} %bitcast.19), calls=%async_computation.1 | async-start | bytes 524288 | tf_op jit(solution)/shard_map/all_to_all | solution.py:61
  126.6 0.0 copy-done.5
  126.6 0.1 reshape.154
  126.7 0.2 convolution_add_fusion
  127.0 448.7 %all-reduce.3.cloned.1.call-done = (f32[256,256]{0,1:T(8,128)}, f32[256,256]{1,0:T(8,128)}) async-done(((f32[256,256]{0,1:T(8,128)}, f32[256,256]{1,0:T(8,128)}), (f32[256,256]{0,1:T(8,128)}, f32[256,256]{1,0:T(8,128)})) %all-reduce.3.cloned.1.call-update) | async-done | bytes 524304 | tf_op jit(solution)/shard_map/psum | solution.py:72
  575.7 1.8 copy.15
  577.5 0.0 all-to-all-done.1
  577.5 0.1 convert_select_fusion
  577.6 0.0 copy-start.4
  577.6 3.4 scatter_fusion.1
  581.1 0.0 reduce-scatter.2.cloned.1.call-done
  581.1 1.0 scatter_fusion.2
  582.1 0.7 convert_element_type.44
  582.8 0.0 copy-done.4
  582.8 0.7 copy.23
  (9 shorter events, 0.1 us)
Async XLA Ops:
  8.0 81.3 %copy-start = (bf16[256,256]{1,0:T(8,128)(2,1)S(1)}, bf16[256,256]{1,0:T(8,128)(2,1)}, u32[]{:S(2)}) copy-start(bf16[256,256]{1,0:T(8,128)(2,1)} %param.11) | copy-start | bytes 393220
  9.6 17.3 %copy-start.6 = (s32[2,8]{1,0:T(2,128)S(1)}, s32[2,8]{1,0:T(2,128)}, u32[]{:S(2)}) copy-start(s32[2,8]{1,0:T(2,128)} %param.13) | copy-start | bytes 196
  9.6 17.4 %copy-start.8 = (s32[1,16]{1,0:T(1,128)S(1)}, s32[1,16]{1,0:T(1,128)}, u32[]{:S(2)}) copy-start(s32[1,16]{1,0:T(1,128)} %param.16) | copy-start | bytes 196
  9.6 17.4 %copy-start.1 = (bf16[256,256]{1,0:T(8,128)(2,1)S(1)}, bf16[256,256]{1,0:T(8,128)(2,1)}, u32[]{:S(2)}) copy-start(bf16[256,256]{1,0:T(8,128)(2,1)} %param.9) | copy-start | bytes 393220
  9.6 18.1 %copy-start.2 = (bf16[2,8,128,128]{3,2,1,0:T(8,128)(2,1)S(1)}, bf16[2,8,128,128]{3,2,1,0:T(8,128)(2,1)}, u32[]{:S(2)}) copy-start(bf16[2,8,128,128]{3,2,1,0:T(8,128)(2,1)} %param.12) | copy-start | bytes 1572868
  12.2 75.9 %copy-start.3 = (bf16[256,256]{1,0:T(8,128)(2,1)S(1)}, bf16[256,256]{1,0:T(8,128)(2,1)}, u32[]{:S(2)}) copy-start(bf16[256,256]{1,0:T(8,128)(2,1)} %param.10) | copy-start | bytes 393220
  13.0 75.3 %all-to-all-start = ((bf16[16,32,256]{2,1,0:T(8,128)(2,1)}), bf16[16,32,256]{2,1,0:T(8,128)(2,1)S(1)}, u32[]{:S(2)}, u32[]{:S(2)}) async-start(bf16[16,32,256]{2,1,0:T(8,128)(2,1)} %broadcast_select_fusion), calls=%async_computation | async-start | bytes 524288 | tf_op jit(solution)/shard_map/all_to_all | solution.py:55
  26.9 548.9 %all-reduce.3.cloned.1.call-start = ((), (), s32[]{:S(2)}) async-start(), calls=%async_computation.4 | async-start | bytes 1048576 | tf_op jit(solution)/shard_map/psum | solution.py:72
  89.0 0.9 copy-start.7
  93.0 488.1 %reduce-scatter.2.cloned.1.call-start = ((), (), s32[]{:S(2)}) async-start(), calls=%async_computation.3 | async-start | bytes 802816 | tf_op jit(solution)/shard_map/reduce_scatter | solution.py:70
  99.0 27.6 %copy-start.5 = (s32[16,32]{1,0:T(8,128)S(1)}, s32[16,32]{1,0:T(8,128)}, u32[]{:S(2)}) copy-start(s32[16,32]{1,0:T(8,128)} %param.14) | copy-start | bytes 6148
  100.7 476.8 %all-to-all-start.1 = ((bf16[16,32,256]{2,1,0:T(8,128)(2,1)}), bf16[16,32,256]{2,1,0:T(8,128)(2,1)S(1)}, u32[]{:S(2)}, u32[]{:S(2)}) async-start(bf16[16,32,256]{2,1,0:T(8,128)(2,1)} %bitcast.19), calls=%async_computation.1 | async-start | bytes 524288 | tf_op jit(solution)/shard_map/all_to_all | solution.py:61
  577.6 5.2 copy-start.4
Sparse Core Ops, SparseCore 0:
  93.2 482.4 all-reduce.2
Sparse Core Ops, SparseCore 1:
  100.1 432.5 reduce-scatter.1
where the time goes:
time: 592 us; the launch traced here: 591 us
  waiting for transfers between devices  449 us (76%)
  blocking collectives  60.2 us (10%)
  starting transfers between devices  39.8 us (7%)
  between operations  15.7 us (3%)
  other arithmetic  11.3 us (2%)
  local copies, waits for them, and re-layouts  11 us (2%)
    psum x1, waiting for transfers between devices, on_device(): grad_self, grad_neigh = lax.psum((grad_ws, grad_wn), ('dom', 'grp'))  449 us
    all_gather x1, blocking collectives, on_device(): hub_feats = lax.all_gather(features[hub_rows[0]], 'grp', axis=0, tiled=True)  60.2 us
    all_to_all x1, starting transfers between devices, on_device(): lax.all_to_all(grad_halo.reshape(outgoing.shape).astype(jnp.bfloat16), 'd...  25.9 us
    all_to_all x1, starting transfers between devices, on_device(): lax.all_to_all(outgoing, 'dom', split_axis=0, concat_axis=0, tiled=True)  13.8 us
  transfers between devices with their start and end apart: 4, of which 1 were waited for; matrix products, arithmetic and copies ran while one was open for 2% of the time, Pallas kernels for 0%

commit v1 on v0

v1 whole, which is shorter than its diff:
```python
import functools

import jax
import jax.numpy as jnp
from jax import lax
from jax.experimental import pallas as pl
from jax.experimental.pallas import tpu as pltpu
from jax.sharding import PartitionSpec as P

CORES = 2
X_CHIPS = 4

F32 = jnp.float32
BF16 = jnp.bfloat16


def mm(a, b):
    return jnp.dot(a, b, preferred_element_type=F32)


def mm_nt(a, b):
    return lax.dot_general(a, b, (((1,), (1,)), ((), ())), preferred_element_type=F32)


def nearest_first(count):
    order = []
    for k in range(1, count // 2 + 1):
        order.append(k)
        if count - k != k:
            order.append(count - k)
    return order


def kernel(
    dims,
    feat, w_self, w_neigh, adj, ids, send_rows, send_counts, hub_rows, cot,
    out, grad_feat, grad_self, grad_neigh,
    out_send, halo_in, hub_in, dense, dense_t, dense_low, dense_low_t, pick, pick_t, feat_t,
    g_send, g_ret, h_send, h_recv, h2_send, h2_recv,
    gw, w_sib, w2_send, w2_recv, w3_send, w3_recv, w4_recv, w_fin,
    halo_s, halo_r, hz_s, hz_r, hx_s, hx_r, gh_s, gh_r, gx_s, gx_r, gz_s, gz_r,
    w1_s, w1_r, w2_s, w2_r, w3_s, w3_r, w4_s, w4_r, w5_s, w5_r, w6_s, w6_r, w7_s, w7_r,
):
    nd, ny, nz, nx = dims
    nodes, width = feat.shape
    row_tiles, per_row, tile, _ = adj.shape
    slots = send_rows.shape[1]
    hubs = hub_rows.shape[1]
    src_tiles = dense.shape[0]
    own_tiles = nodes // tile
    halo_tiles = nd * slots // tile
    crows = w_fin.shape[3]
    me_d = lax.axis_index("dom")
    me_g = lax.axis_index("grp")
    y, core = lax.div(me_d, CORES), lax.rem(me_d, CORES)
    z, x = lax.div(me_g, nx), lax.rem(me_g, nx)

    def dom_at(k):
        return lax.rem(me_d + k, nd)

    def z_at(k):
        return lax.rem(z + k, nz)

    def x_at(k):
        return lax.rem(x + k, nx)

    def y_at(k):
        return lax.rem(y + k, ny)

    sibling = y * CORES + (1 - core)
    pending = []

    def push(src, dst, send_sem, recv_sem, d, g):
        copy = pltpu.make_async_remote_copy(
            src_ref=src, dst_ref=dst, send_sem=send_sem, recv_sem=recv_sem,
            device_id=(d, g), device_id_type=pl.DeviceIdType.MESH,
        )
        copy.start()
        pending.append(copy)
        return copy

    barrier = pltpu.get_barrier_semaphore()
    partners = [(dom_at(k), me_g) for k in range(1, nd)]
    partners += [(me_d, z_at(k) * nx + x) for k in range(1, nz)]
    partners += [(me_d, z * nx + x_at(k)) for k in range(1, nx)]
    for partner in partners:
        pl.semaphore_signal(barrier, inc=1, device_id=partner, device_id_type=pl.DeviceIdType.MESH)

    count_col = jnp.sum(
        jnp.where(
            lax.broadcasted_iota(jnp.int32, (nd, nd), 0) == lax.broadcasted_iota(jnp.int32, (nd, nd), 1),
            jnp.broadcast_to(send_counts[...], (nd, nd)), 0).astype(F32),
        axis=1, keepdims=True)
    live = lax.broadcasted_iota(jnp.int32, (nd, slots), 1).astype(F32) < count_col
    index = jnp.where(live, send_rows[...].astype(F32), -1.0)
    eye = lax.broadcasted_iota(jnp.int32, (slots, slots), 0) == lax.broadcasted_iota(jnp.int32, (slots, slots), 1)
    lane = lax.broadcasted_iota(jnp.int32, (slots, nodes), 1).astype(F32)
    for p in range(nd):
        column = jnp.sum(
            jnp.where(eye, jnp.broadcast_to(index[p:p + 1, :], (slots, slots)), 0.0), axis=1, keepdims=True)
        pick[p * slots:(p + 1) * slots, :] = jnp.where(lane == column, 1.0, 0.0).astype(BF16)
    hub_index = hub_rows[...].astype(F32)
    hub_eye = lax.broadcasted_iota(jnp.int32, (hubs, hubs), 0) == lax.broadcasted_iota(jnp.int32, (hubs, hubs), 1)
    hub_col = jnp.sum(
        jnp.where(hub_eye, jnp.broadcast_to(hub_index, (hubs, hubs)), 0.0), axis=1, keepdims=True)
    hub_pick = jnp.where(
        lax.broadcasted_iota(jnp.int32, (hubs, nodes), 1).astype(F32) == hub_col, 1.0, 0.0).astype(BF16)
    features = feat[...]
    hub_in[z, x] = mm(hub_pick, features).astype(BF16)
    out_send[...] = mm(pick[...], features).astype(BF16).reshape(nd, slots, width)
    halo_in[me_d] = out_send[me_d]

    pl.semaphore_wait(barrier, len(partners))

    near_z = nearest_first(nz)
    hub_z = {}
    for k in reversed(near_z):
        hub_z[k] = push(hub_in.at[z, x], hub_in.at[z, x], hz_s.at[k], hz_r.at[k], me_d, z_at(k) * nx + x)
    hub_x = []

    def forward(k):
        from_z = lax.rem(z + nz - k, nz)
        for j in range(1, nx):
            hub_x.append(push(
                hub_in.at[from_z, x], hub_in.at[from_z, x], hx_s.at[j, k], hx_r.at[j, k], me_d, z * nx + x_at(j)))

    forward(0)
    halo = []
    for k in range(1, nd):
        halo.append(push(
            out_send.at[dom_at(k)], halo_in.at[me_d], halo_s.at[k], halo_r.at[k], dom_at(k), me_g))

    def gather_tiles(c, carry):
        parts = []
        for r in range(row_tiles):
            total = jnp.zeros((tile, tile), F32)
            for t in range(per_row):
                total = total + jnp.where(ids[r, t] == c, adj[r, t].astype(F32), 0.0)
            parts.append(total)
        block = jnp.concatenate(parts, axis=0)
        high = block.astype(BF16)
        low = block - high.astype(F32)
        dense[c] = high
        dense_low[c] = low.astype(BF16)
        dense_t[c] = high.astype(F32).T.astype(BF16)
        dense_low_t[c] = low.T.astype(BF16)
        return carry

    lax.fori_loop(0, src_tiles, gather_tiles, 0)

    for k in near_z:
        hub_z[k].wait_recv()
        forward(k)

    sums = []
    for r in range(row_tiles):
        total = jnp.zeros((tile, tile), F32)
        for t in range(per_row):
            total = total + adj[r, t].astype(F32)
        sums.append(jnp.sum(total, axis=1, keepdims=True))
    inverse = 1.0 / (1.0 + jnp.concatenate(sums, axis=0))
    feat_t[...] = features.astype(F32).T.astype(BF16)
    pick_t[...] = pick[...].astype(F32).T.astype(BF16)

    def from_tiles(first, count, rows):
        return sum(
            mm(jnp.concatenate([part[c] for c in range(first, first + count)], axis=1), rows)
            for part in (dense, dense_low))

    def to_tiles(first, count, rows):
        return sum(
            mm(part[first:first + count].reshape(count * tile, nodes), rows) for part in (dense_t, dense_low_t))

    numer = from_tiles(0, own_tiles, features)
    pre = mm(features, w_self[...])
    for copy in halo:
        copy.wait_recv()
    numer = numer + from_tiles(own_tiles, halo_tiles, halo_in[...].reshape(nd * slots, width))
    for copy in hub_x:
        copy.wait_recv()
    hub_tiles = src_tiles - own_tiles - halo_tiles
    numer = numer + from_tiles(own_tiles + halo_tiles, hub_tiles, hub_in[...].reshape(nz * nx * hubs, width))
    agg = numer * inverse
    agg_b = agg.astype(BF16)
    pre = pre + mm(agg_b, w_neigh[...])
    sig = 1.0 / (1.0 + jnp.exp(-pre))
    out[...] = (pre * sig).astype(BF16)
    grad_pre = (cot[...].astype(F32) * sig * (1.0 + pre * (1.0 - sig))).astype(BF16)

    gw[0] = mm(feat_t[...], grad_pre)
    gw[1] = mm(agg_b.astype(F32).T.astype(BF16), grad_pre)
    w1 = push(gw.at[1 - core], w_sib, w1_s, w1_r, sibling, me_g)

    grad_num = (mm_nt(grad_pre, w_neigh[...]) * inverse).astype(BF16)
    hub_grad = to_tiles(own_tiles + halo_tiles, hub_tiles, grad_num).astype(BF16)
    for g in range(nz * nx):
        h_send[g % nx, g // nx] = hub_grad[g * hubs:(g + 1) * hubs, :]
    hub_gx = [
        push(h_send.at[x_at(j)], h_recv.at[x], gx_s.at[j], gx_r.at[j], me_d, z * nx + x_at(j)) for j in range(1, nx)]
    h_recv[x] = h_send[x]
    g_send[...] = to_tiles(own_tiles, halo_tiles, grad_num).astype(BF16).reshape(nd, slots, width)

    w1.wait_recv()
    mine = gw[core] + w_sib[...]
    yrows = nodes // ny
    for i in range(ny):
        for j in range(nx):
            top = i * yrows + (j // 2) * crows
            w2_send[i, j] = mine[top:top + crows, (j % 2) * 128:(j % 2) * 128 + 128].astype(BF16)
    w2 = [
        push(w2_send.at[y_at(k)], w2_recv.at[y], w2_s.at[k], w2_r.at[k], y_at(k) * CORES + core, me_g)
        for k in range(1, ny)]
    w2_recv[y] = w2_send[y]
    ret = [
        push(g_send.at[dom_at(k)], g_ret.at[me_d], gh_s.at[k], gh_r.at[k], dom_at(k), me_g) for k in range(1, nd)]
    g_ret[me_d] = g_send[me_d]
    own_grad = mm_nt(grad_pre, w_self[...]) + to_tiles(0, own_tiles, grad_num)

    for copy in w2:
        copy.wait_recv()
    total = w2_recv[0].astype(F32)
    for i in range(1, ny):
        total = total + w2_recv[i].astype(F32)
    w3_send[...] = total
    w3 = [
        push(w3_send.at[x_at(j)], w3_recv.at[x], w3_s.at[j], w3_r.at[j], me_d, z * nx + x_at(j)) for j in range(1, nx)]
    w3_recv[x] = w3_send[x]

    for copy in hub_gx:
        copy.wait_recv()
    total = h_recv[0].astype(F32)
    for j in range(1, nx):
        total = total + h_recv[j].astype(F32)
    h2_send[...] = total.astype(BF16)
    hub_gz = [
        push(h2_send.at[z_at(k)], h2_recv.at[z], gz_s.at[k], gz_r.at[k], me_d, z_at(k) * nx + x) for k in range(1, nz)]
    h2_recv[z] = h2_send[z]

    for copy in w3:
        copy.wait_recv()
    total = w3_recv[0]
    for j in range(1, nx):
        total = total + w3_recv[j]
    w4_recv[z] = total.astype(BF16)
    w4 = [
        push(w4_recv.at[z], w4_recv.at[z], w4_s.at[k], w4_r.at[k], me_d, z_at(k) * nx + x) for k in range(1, nz)]

    for copy in ret:
        copy.wait_recv()
    own_grad = own_grad + mm(pick_t[...], g_ret[...].reshape(nd * slots, width))

    for copy in w4:
        copy.wait_recv()
    total = w4_recv[0].astype(F32)
    for k in range(1, nz):
        total = total + w4_recv[k].astype(F32)
    w_fin[core, x, y] = total.astype(BF16)
    w5 = [
        push(w_fin.at[core, x, y], w_fin.at[core, x, y], w5_s.at[k], w5_r.at[k], y_at(k) * CORES + core, me_g)
        for k in range(1, ny)]

    for copy in hub_gz:
        copy.wait_recv()
    hub_total = h2_recv[0].astype(F32)
    for k in range(1, nz):
        hub_total = hub_total + h2_recv[k].astype(F32)
    hub_pick_t = jnp.where(
        lax.broadcasted_iota(jnp.int32, (nodes, hubs), 0).astype(F32) == jnp.broadcast_to(hub_index, (nodes, hubs)),
        1.0, 0.0).astype(BF16)
    high = hub_total.astype(BF16)
    low = (hub_total - high.astype(F32)).astype(BF16)
    grad_feat[...] = (own_grad + mm(hub_pick_t, high) + mm(hub_pick_t, low)).astype(BF16)

    for copy in w5:
        copy.wait_recv()
    w6 = [
        push(w_fin.at[core, x], w_fin.at[core, x], w6_s.at[j], w6_r.at[j], me_d, z * nx + x_at(j))
        for j in range(1, nx)]
    w7 = [push(w_fin.at[core, x], w_fin.at[core, x], w7_s.at[0], w7_r.at[0], sibling, me_g)]
    for j in range(1, nx):
        w6[j - 1].wait_recv()
        from_x = lax.rem(x + nx - j, nx)
        w7.append(push(w_fin.at[core, from_x], w_fin.at[core, from_x], w7_s.at[j], w7_r.at[j], sibling, me_g))
    for copy in w7:
        copy.wait_recv()
    for matrix, result in enumerate((grad_self, grad_neigh)):
        for j in range(nx):
            for i in range(ny):
                top = i * yrows + (j // 2) * crows
                result[top:top + crows, (j % 2) * 128:(j % 2) * 128 + 128] = w_fin[matrix, j, i].astype(F32)

    for copy in pending:
        copy.wait_send()


def on_device(dims, features, w_self, w_neigh, adjacency, tile_ids, send_rows, send_counts, hub_rows, cotangent):
    nd, ny, nz, nx = dims
    nodes, width = features.shape
    row_tiles, _, tile, _ = adjacency.shape
    slots, hubs = send_rows.shape[1], hub_rows.shape[1]
    src_tiles = (nodes + nd * slots + nz * nx * hubs) // tile
    crows = nodes // ny // (nx // 2)
    vmem = pl.BlockSpec(memory_space=pltpu.VMEM)
    smem = pl.BlockSpec(memory_space=pltpu.SMEM)
    dma = pltpu.SemaphoreType.DMA
    pairs = [(nd,), (nz,), (nx, nz), (nd,), (nx,), (nz,), (), (ny,), (nx,), (nz,), (ny,), (nx,), (nx,)]
    return pl.pallas_call(
        functools.partial(kernel, dims),
        out_shape=(
            jax.ShapeDtypeStruct((nodes, width), BF16),
            jax.ShapeDtypeStruct((nodes, width), BF16),
            jax.ShapeDtypeStruct((width, width), F32),
            jax.ShapeDtypeStruct((width, width), F32),
        ),
        in_specs=[vmem, vmem, vmem, vmem, smem, vmem, vmem, vmem, vmem],
        out_specs=[vmem] * 4,
        scratch_shapes=[
            pltpu.VMEM((nd, slots, width), BF16),
            pltpu.VMEM((nd, slots, width), BF16),
            pltpu.VMEM((nz, nx, hubs, width), BF16),
            pltpu.VMEM((src_tiles, nodes, tile), BF16),
            pltpu.VMEM((src_tiles, tile, nodes), BF16),
            pltpu.VMEM((src_tiles, nodes, tile), BF16),
            pltpu.VMEM((src_tiles, tile, nodes), BF16),
            pltpu.VMEM((nd * slots, nodes), BF16),
            pltpu.VMEM((nodes, nd * slots), BF16),
            pltpu.VMEM((width, nodes), BF16),
            pltpu.VMEM((nd, slots, width), BF16),
            pltpu.VMEM((nd, slots, width), BF16),
            pltpu.VMEM((nx, nz, hubs, width), BF16),
            pltpu.VMEM((nx, nz, hubs, width), BF16),
            pltpu.VMEM((nz, hubs, width), BF16),
            pltpu.VMEM((nz, hubs, width), BF16),
            pltpu.VMEM((2, width, width), F32),
            pltpu.VMEM((width, width), F32),
            pltpu.VMEM((ny, nx, crows, 128), BF16),
            pltpu.VMEM((ny, nx, crows, 128), BF16),
            pltpu.VMEM((nx, crows, 128), F32),
            pltpu.VMEM((nx, crows, 128), F32),
            pltpu.VMEM((nz, crows, 128), BF16),
            pltpu.VMEM((2, nx, ny, crows, 128), BF16),
        ] + [dma(shape) for shape in pairs for _ in range(2)],
        compiler_params=pltpu.CompilerParams(
            collective_id=0, has_side_effects=True, vmem_limit_bytes=40 * 1024 * 1024),
    )(features, w_self, w_neigh, adjacency, tile_ids, send_rows, send_counts, hub_rows, cotangent)


def solution(mesh):
    nd, ng = mesh.shape["dom"], mesh.shape["grp"]
    dims = (nd, nd // CORES, ng // X_CHIPS, X_CHIPS)
    placed = (
        P(("dom", "grp"), None),
        P(),
        P(),
        P(("dom", "grp"), None, None, None),
        P(("dom", "grp"), None),
        P(("dom", "grp"), None),
        P(("dom", "grp"), None),
        P(("dom", "grp"), None),
        P(("dom", "grp"), None),
    )
    return jax.shard_map(
        functools.partial(on_device, dims),
        mesh=mesh,
        in_specs=placed,
        out_specs=(P(("dom", "grp"), None), P(("dom", "grp"), None), P(), P()),
        check_vma=False,
    )
```

time: 592 us -> 74 us (0.12)
  waiting for transfers between devices: 449 us -> 0 us
  Pallas kernels: 0 us -> 62.9 us
  blocking collectives: 60.2 us -> 0 us
  starting transfers between devices: 39.8 us -> 0 us
  between operations: 15.7 us -> 0.66 us
  other arithmetic: 11.3 us -> 0 us
    psum x1 -> x0, waiting for transfers between devices: 449 us -> none  [on_device(): grad_self, grad_neigh = lax.psum((grad_ws, grad_wn), ('dom', 'grp'))]
    pallas_call x0 -> x1, Pallas kernels: none -> 62.9 us  [on_device(): pl.pallas_call(functools.partial(kernel, dims), out_shape=(jax.ShapeDtype...]
    all_gather x1 -> x0, blocking collectives: 60.2 us -> none  [on_device(): hub_feats = lax.all_gather(features[hub_rows[0]], 'grp', axis=0, tiled=True)]
    all_to_all x2 -> x0, starting transfers between devices: 39.7 us -> none  [the longest x1 25.9 us: on_device(): lax.all_to_all(grad_halo.reshape(outgoing.shape).astype(jnp.bfloat16), 'd...]
    scatter-add x3 -> x0, other arithmetic: 7.94 us -> none  [the longest x1 3.5 us: local_layer(): grad_source = jnp.zeros((src_count, tile_size, feat_width), jnp.float32)....]
    unnamed x20 -> x22, local copies, waits for them, and re-layouts: 3.11 us -> 10.1 us
  transfers between devices with their start and end apart: 4 -> 0, of which waited for: 1 -> 0; matrix products, arithmetic and copies ran while one was open for 2% -> 0% of each run, Pallas kernels for 0% -> 0%
where the time goes in v1:
time: 74 us; the launch traced here: 73.7 us
  Pallas kernels  62.9 us (85%)
  local copies, waits for them, and re-layouts  10.1 us (14%)
    pallas_call x1, Pallas kernels, on_device(): pl.pallas_call(functools.partial(kernel, dims), out_shape=(jax.ShapeDtype...  62.9 us
    unnamed x22, local copies, waits for them, and re-layouts  10.1 us

profile of v1, /device:TPU:1, one launch (start us, length us, event | category | flops | bytes accessed | tf_op | source)
XLA Modules:
  0.0 73.7 jit_solution(15637248829442521406)
XLA Ops:
  0.6 0.0 copy-start
  0.6 1.0 %copy-done = bf16[2,8,128,128]{3,2,1,0:T(8,128)(2,1)S(1)} copy-done((bf16[2,8,128,128]{3,2,1,0:T(8,128)(2,1)S(1)}, bf16[2,8,128,128]{3,2,1,0:T(8,128)(2,1)}, u32[]{:S(2)}) %copy-start) | copy-done | bytes 524312
  1.7 0.0 copy-start.1
  1.7 0.9 %copy-done.1 = bf16[256,256]{1,0:T(8,128)(2,1)S(1)} copy-done((bf16[256,256]{1,0:T(8,128)(2,1)S(1)}, bf16[256,256]{1,0:T(8,128)(2,1)}, u32[]{:S(2)}) %copy-start.1) | copy-done | bytes 131096
  2.6 0.0 copy-start.2
  2.6 0.9 %copy-done.2 = bf16[256,256]{1,0:T(8,128)(2,1)S(1)} copy-done((bf16[256,256]{1,0:T(8,128)(2,1)S(1)}, bf16[256,256]{1,0:T(8,128)(2,1)}, u32[]{:S(2)}) %copy-start.2) | copy-done | bytes 131096
  3.5 0.0 copy-start.3
  3.5 0.9 %copy-done.3 = bf16[256,256]{1,0:T(8,128)(2,1)S(1)} copy-done((bf16[256,256]{1,0:T(8,128)(2,1)S(1)}, bf16[256,256]{1,0:T(8,128)(2,1)}, u32[]{:S(2)}) %copy-start.3) | copy-done | bytes 131096
  4.4 0.0 copy-start.4
  4.4 0.9 %copy-done.4 = bf16[256,256]{1,0:T(8,128)(2,1)S(1)} copy-done((bf16[256,256]{1,0:T(8,128)(2,1)S(1)}, bf16[256,256]{1,0:T(8,128)(2,1)}, u32[]{:S(2)}) %copy-start.4) | copy-done | bytes 131096
  5.3 0.0 copy-start.5
  5.3 0.7 copy-done.5
  6.0 0.0 copy-start.6
  6.0 0.7 copy-done.6
  6.7 0.0 copy-start.7
  6.7 0.7 copy-done.7
  7.3 0.0 copy-start.8
  7.3 0.7 copy-done.8
  8.0 62.9 %shard_map.120 = (bf16[256,256]{1,0:T(8,128)(2,1)S(1)}, bf16[256,256]{1,0:T(8,128)(2,1)S(1)}, f32[256,256]{1,0:T(8,128)S(1)}, f32[256,256]{1,0:T(8,128)S(1)}) custom-call(bf16[256,256]{1,0:T(8,128)(2,1)S(1)} %copy-done.1, bf16[256,256]{1,0:T(8,128)(2,1)S(1)} %copy-done.2, bf16[256,256]{1,0:T(8,128)(2,1)S(1)} %copy-done.3, ...), custom_call_target="tpu_custom_call" | custom-call | tf_op jit(solution)/shard_map/pallas_call | solution.py:307
  70.9 0.7 copy.17
  71.6 0.7 copy.18
  72.3 0.7 copy.19
  73.0 0.7 copy.20
Async XLA Ops:
  0.6 1.0 %copy-start = (bf16[2,8,128,128]{3,2,1,0:T(8,128)(2,1)S(1)}, bf16[2,8,128,128]{3,2,1,0:T(8,128)(2,1)}, u32[]{:S(2)}) copy-start(bf16[2,8,128,128]{3,2,1,0:T(8,128)(2,1)} %adj.1) | copy-start | bytes 1572868
  1.7 0.9 %copy-start.1 = (bf16[256,256]{1,0:T(8,128)(2,1)S(1)}, bf16[256,256]{1,0:T(8,128)(2,1)}, u32[]{:S(2)}) copy-start(bf16[256,256]{1,0:T(8,128)(2,1)} %feat.1) | copy-start | bytes 393220
  2.6 0.9 %copy-start.2 = (bf16[256,256]{1,0:T(8,128)(2,1)S(1)}, bf16[256,256]{1,0:T(8,128)(2,1)}, u32[]{:S(2)}) copy-start(bf16[256,256]{1,0:T(8,128)(2,1)} %w_self.1) | copy-start | bytes 393220
  3.5 0.9 %copy-start.3 = (bf16[256,256]{1,0:T(8,128)(2,1)S(1)}, bf16[256,256]{1,0:T(8,128)(2,1)}, u32[]{:S(2)}) copy-start(bf16[256,256]{1,0:T(8,128)(2,1)} %w_neigh.1) | copy-start | bytes 393220
  4.4 0.9 %copy-start.4 = (bf16[256,256]{1,0:T(8,128)(2,1)S(1)}, bf16[256,256]{1,0:T(8,128)(2,1)}, u32[]{:S(2)}) copy-start(bf16[256,256]{1,0:T(8,128)(2,1)} %cot.1) | copy-start | bytes 393220
  5.3 0.7 copy-start.5
  6.0 0.7 copy-start.6
  6.7 0.7 copy-start.7
  7.3 0.7 copy-start.8

commit v2 on v1

v2 whole, which is shorter than its diff:
```python
import functools

import jax
import jax.numpy as jnp
from jax import lax
from jax.experimental import pallas as pl
from jax.experimental.pallas import tpu as pltpu
from jax.sharding import PartitionSpec as P

CORES = 2
X_CHIPS = 4

VMEM_LIMIT = 60 * 1024 * 1024

F32 = jnp.float32
BF16 = jnp.bfloat16


def mm(a, b):
    return jnp.dot(a, b, preferred_element_type=F32)


def mm_nt(a, b):
    return lax.dot_general(a, b, (((1,), (1,)), ((), ())), preferred_element_type=F32)


def far_first(*sizes):
    offsets = [()]
    for size in sizes:
        offsets = [o + (k,) for o in offsets for k in range(size)]
    hops = lambda o: sum(min(k, size - k) for k, size in zip(o, sizes))
    return sorted((o for o in offsets if any(o)), key=lambda o: -hops(o))


def kernel(
    dims,
    feat_in, w_self_in, w_neigh_in, adj_in, ids_in, send_rows_in, send_counts_in, hub_rows_in, cot_in,
    out_to, grad_feat_to, w_fin_to,
    feat, w_self, w_neigh, adj, ids, send_rows, send_counts, hub_rows, cot, load_sem,
    out, grad_feat, store_sem,
    out_send, halo_in, hub_in, dense, dense_t, dense_low, dense_low_t, pick, pick_t, lhs_t,
    g_send, g_ret, h_send, h_recv, h2_send, h2_recv,
    gw, w_sib, w2_send, w2_recv, w4_recv, w_fin,
    halo_s, halo_r, hz_s, hz_r, hx_s, hx_r, gh_s, gh_r, gx_s, gx_r, gz_s, gz_r,
    w1_s, w1_r, w2_s, w2_r, w4_s, w4_r, w5_s, w5_r, w7_s, w7_r,
):
    nd, ny, nz, nx = dims
    nodes, width = feat.shape
    row_tiles, per_row, tile, _ = adj.shape
    slots = send_rows.shape[1]
    hubs = hub_rows.shape[1]
    src_tiles = dense.shape[0]
    own_tiles = nodes // tile
    halo_tiles = nd * slots // tile
    crows = w_fin.shape[3]
    me_d = lax.axis_index("dom")
    me_g = lax.axis_index("grp")
    y, core = lax.div(me_d, CORES), lax.rem(me_d, CORES)
    z, x = lax.div(me_g, nx), lax.rem(me_g, nx)

    def dom_at(k):
        return lax.rem(me_d + k, nd)

    def z_at(k):
        return lax.rem(z + k, nz)

    def x_at(k):
        return lax.rem(x + k, nx)

    def y_at(k):
        return lax.rem(y + k, ny)

    sibling = y * CORES + (1 - core)
    pending = []

    def push(src, dst, send_sem, recv_sem, d, g):
        copy = pltpu.make_async_remote_copy(
            src_ref=src, dst_ref=dst, send_sem=send_sem, recv_sem=recv_sem,
            device_id=(d, g), device_id_type=pl.DeviceIdType.MESH,
        )
        copy.start()
        pending.append(copy)
        return copy

    def arrive(*copies):
        for copy in copies:
            copy.wait_recv()

    loads = [
        pltpu.make_async_copy(src, dst, load_sem.at[i])
        for i, (src, dst) in enumerate((
            (hub_rows_in, hub_rows), (feat_in, feat), (send_counts_in, send_counts), (send_rows_in, send_rows),
            (ids_in, ids), (adj_in, adj), (w_self_in, w_self), (w_neigh_in, w_neigh), (cot_in, cot)))
    ]
    for load in loads:
        load.start()

    barrier = pltpu.get_barrier_semaphore()
    partners = [(dom_at(k), me_g) for k in range(1, nd)]
    partners += [(me_d, z_at(k) * nx + x) for k in range(1, nz)]
    partners += [(me_d, z * nx + x_at(k)) for k in range(1, nx)]
    for partner in partners:
        pl.semaphore_signal(barrier, inc=1, device_id=partner, device_id_type=pl.DeviceIdType.MESH)

    far = max(1, nz // 3)
    far_z = [k for (k,) in far_first(nz)]
    far_x = [k for (k,) in far_first(nx)]
    own_slot = nz - far
    for load in loads[:2]:
        load.wait()
    features = feat[...]
    hub_index = hub_rows[...].astype(F32)
    hub_eye = lax.broadcasted_iota(jnp.int32, (hubs, hubs), 0) == lax.broadcasted_iota(jnp.int32, (hubs, hubs), 1)
    hub_col = jnp.sum(
        jnp.where(hub_eye, jnp.broadcast_to(hub_index, (hubs, hubs)), 0.0), axis=1, keepdims=True)
    hub_pick = jnp.where(
        lax.broadcasted_iota(jnp.int32, (hubs, nodes), 1).astype(F32) == hub_col, 1.0, 0.0).astype(BF16)
    hub_in[x, own_slot] = mm(hub_pick, features).astype(BF16)

    pl.semaphore_wait(barrier, len(partners))

    hub_z = {}
    for k in far_z:
        hub_z[k] = push(
            hub_in.at[x, own_slot], hub_in.at[x, (k - far) % nz], hz_s.at[k], hz_r.at[k], me_d, z_at(k) * nx + x)
    hub_x = []

    def forward(group, first, last):
        block = hub_in.at[x, pl.ds(first, last - first)]
        for j in far_x:
            hub_x.append(push(block, block, hx_s.at[j, group], hx_r.at[j, group], me_d, z * nx + x_at(j)))

    forward(0, own_slot, own_slot + 1)

    for load in loads[2:4]:
        load.wait()
    count_col = jnp.sum(
        jnp.where(
            lax.broadcasted_iota(jnp.int32, (nd, nd), 0) == lax.broadcasted_iota(jnp.int32, (nd, nd), 1),
            jnp.broadcast_to(send_counts[...], (nd, nd)), 0).astype(F32),
        axis=1, keepdims=True)
    live = lax.broadcasted_iota(jnp.int32, (nd, slots), 1).astype(F32) < count_col
    index = jnp.where(live, send_rows[...].astype(F32), -1.0)
    eye = lax.broadcasted_iota(jnp.int32, (slots, slots), 0) == lax.broadcasted_iota(jnp.int32, (slots, slots), 1)
    lane = lax.broadcasted_iota(jnp.int32, (slots, nodes), 1).astype(F32)
    for p in range(nd):
        column = jnp.sum(
            jnp.where(eye, jnp.broadcast_to(index[p:p + 1, :], (slots, slots)), 0.0), axis=1, keepdims=True)
        pick[p * slots:(p + 1) * slots, :] = jnp.where(lane == column, 1.0, 0.0).astype(BF16)
    out_send[...] = mm(pick[...], features).astype(BF16).reshape(nd, slots, width)
    halo_in[me_d] = out_send[me_d]
    far_dom = [i * CORES + j for i, j in far_first(ny, CORES)]
    halo = [
        push(out_send.at[dom_at(k)], halo_in.at[me_d], halo_s.at[k], halo_r.at[k], dom_at(k), me_g) for k in far_dom]

    def gather_tiles(c, carry):
        parts = []
        for r in range(row_tiles):
            total = jnp.zeros((tile, tile), F32)
            for t in range(per_row):
                total = total + jnp.where(ids[r, t] == c, adj[r, t].astype(F32), 0.0)
            parts.append(total)
        block = jnp.concatenate(parts, axis=0)
        high = block.astype(BF16)
        low = block - high.astype(F32)
        dense[c] = high
        dense_low[c] = low.astype(BF16)
        dense_t[c] = high.astype(F32).T.astype(BF16)
        dense_low_t[c] = low.T.astype(BF16)
        return carry

    for load in loads[4:]:
        load.wait()
    lax.fori_loop(0, src_tiles, gather_tiles, 0)

    arrive(*[hub_z[k] for k in range(far, nz - far + 1)])
    forward(1, 0, nz - 2 * far + 1)
    arrive(*[hub_z[k] for k in far_z if not far <= k <= nz - far])
    if far > 1:
        forward(2, nz - 2 * far + 1, own_slot)
        forward(3, own_slot + 1, nz)

    sums = []
    for r in range(row_tiles):
        total = jnp.zeros((tile, tile), F32)
        for t in range(per_row):
            total = total + adj[r, t].astype(F32)
        sums.append(jnp.sum(total, axis=1, keepdims=True))
    inverse = 1.0 / (1.0 + jnp.concatenate(sums, axis=0))
    lhs_t[0] = features.astype(F32).T.astype(BF16)
    pick_t[...] = pick[...].astype(F32).T.astype(BF16)

    def from_tiles(first, count, rows):
        return sum(
            mm(jnp.concatenate([part[c] for c in range(first, first + count)], axis=1), rows)
            for part in (dense, dense_low))

    def to_tiles(first, count, rows):
        return sum(
            mm(part[first:first + count].reshape(count * tile, nodes), rows) for part in (dense_t, dense_low_t))

    numer = from_tiles(0, own_tiles, features)
    pre = mm(features, w_self[...])
    arrive(*halo)
    numer = numer + from_tiles(own_tiles, halo_tiles, halo_in[...].reshape(nd * slots, width))
    arrive(*hub_x)
    hub_rows_all = jnp.concatenate(
        [hub_in[j, lax.rem(z - i - far + 2 * nz, nz)] for i in range(nz) for j in range(nx)], axis=0)
    hub_tiles = src_tiles - own_tiles - halo_tiles
    numer = numer + from_tiles(own_tiles + halo_tiles, hub_tiles, hub_rows_all)
    agg = numer * inverse
    agg_b = agg.astype(BF16)
    pre = pre + mm(agg_b, w_neigh[...])
    sig = 1.0 / (1.0 + jnp.exp(-pre))
    out[...] = (pre * sig).astype(BF16)
    stores = [pltpu.make_async_copy(out, out_to, store_sem.at[0])]
    stores[-1].start()
    grad_pre = (cot[...].astype(F32) * sig * (1.0 + pre * (1.0 - sig))).astype(BF16)

    lhs_t[1] = agg_b.astype(F32).T.astype(BF16)
    gw[...] = mm(lhs_t[1 - core], grad_pre)
    w1 = push(gw, w_sib, w1_s, w1_r, sibling, me_g)
    mine = mm(lhs_t[core], grad_pre)

    grad_num = (mm_nt(grad_pre, w_neigh[...]) * inverse).astype(BF16)
    hub_grad = to_tiles(own_tiles + halo_tiles, hub_tiles, grad_num).astype(BF16)
    for g in range(nz * nx):
        h_send[g % nx, g // nx] = hub_grad[g * hubs:(g + 1) * hubs, :]
    g_send[...] = to_tiles(own_tiles, halo_tiles, grad_num).astype(BF16).reshape(nd, slots, width)

    arrive(w1)
    mine = mine + w_sib[...]
    yrows = nodes // ny
    plane = far_first(ny, nx)
    for i in range(ny):
        for j in range(nx):
            top = i * yrows + (j // 2) * crows
            w2_send[i, j] = mine[top:top + crows, (j % 2) * 128:(j % 2) * 128 + 128].astype(BF16)
    w2 = [
        push(w2_send.at[y_at(i), x_at(j)], w2_recv.at[n + 1], w2_s.at[n], w2_r.at[n], y_at(i) * CORES + core,
             z * nx + x_at(j)) for n, (i, j) in enumerate(plane)]
    w2_recv[0] = w2_send[y, x]
    hub_gx = [
        push(h_send.at[x_at(j)], h_recv.at[x], gx_s.at[j], gx_r.at[j], me_d, z * nx + x_at(j)) for j in far_x]
    h_recv[x] = h_send[x]
    own_grad = mm_nt(grad_pre, w_self[...]) + to_tiles(0, own_tiles, grad_num)

    arrive(*w2)
    w4_recv[z] = jnp.sum(w2_recv[...].astype(F32), axis=0).astype(BF16)
    w4 = [
        push(w4_recv.at[z], w4_recv.at[z], w4_s.at[k], w4_r.at[k], me_d, z_at(k) * nx + x) for k in far_z]
    ret = [
        push(g_send.at[dom_at(k)], g_ret.at[me_d], gh_s.at[k], gh_r.at[k], dom_at(k), me_g) for k in far_dom]
    g_ret[me_d] = g_send[me_d]

    arrive(*hub_gx)
    h2_send[...] = jnp.sum(h_recv[...].astype(F32), axis=0).astype(BF16)

    arrive(*w4)
    w_fin[core, x, y] = jnp.sum(w4_recv[...].astype(F32), axis=0).astype(BF16)
    w5 = [
        push(w_fin.at[core, x, y], w_fin.at[core, x, y], w5_s.at[n], w5_r.at[n], y_at(i) * CORES + core,
             z * nx + x_at(j)) for n, (i, j) in enumerate(plane)]
    hub_gz = [
        push(h2_send.at[z_at(k)], h2_recv.at[z], gz_s.at[k], gz_r.at[k], me_d, z_at(k) * nx + x) for k in far_z]
    h2_recv[z] = h2_send[z]

    arrive(*ret)
    own_grad = own_grad + mm(pick_t[...], g_ret[...].reshape(nd * slots, width))

    arrive(*w5)
    w7 = push(w_fin.at[core], w_fin.at[core], w7_s, w7_r, sibling, me_g)

    arrive(*hub_gz)
    hub_total = jnp.sum(h2_recv[...].astype(F32), axis=0)
    hub_pick_t = jnp.where(
        lax.broadcasted_iota(jnp.int32, (nodes, hubs), 0).astype(F32) == jnp.broadcast_to(hub_index, (nodes, hubs)),
        1.0, 0.0).astype(BF16)
    high = hub_total.astype(BF16)
    low = (hub_total - high.astype(F32)).astype(BF16)
    grad_feat[...] = (own_grad + mm(hub_pick_t, high) + mm(hub_pick_t, low)).astype(BF16)
    stores.append(pltpu.make_async_copy(grad_feat, grad_feat_to, store_sem.at[1]))
    stores[-1].start()

    arrive(w7)
    stores.append(pltpu.make_async_copy(w_fin, w_fin_to, store_sem.at[2]))
    stores[-1].start()
    for copy in pending:
        copy.wait_send()
    for copy in stores:
        copy.wait()


def store(out_in, grad_in, w_in, out_to, grad_to, self_to, neigh_to, out, grad, w_fin, grad_self, grad_neigh, load_sem, store_sem):
    loads = [
        pltpu.make_async_copy(src, via, load_sem.at[i])
        for i, (src, via) in enumerate(((w_in, w_fin), (out_in, out), (grad_in, grad)))]
    stores = [
        pltpu.make_async_copy(via, dst, store_sem.at[i])
        for i, (via, dst) in enumerate(((grad_self, self_to), (grad_neigh, neigh_to), (out, out_to), (grad, grad_to)))]
    for load in loads:
        load.start()
    for load in loads:
        load.wait()
    stores[2].start()
    stores[3].start()
    _, nx, ny, crows, _ = w_fin.shape
    for matrix, result in enumerate((grad_self, grad_neigh)):
        for j in range(nx):
            for i in range(ny):
                top = (i * (nx // 2) + j // 2) * crows
                result[top:top + crows, (j % 2) * 128:(j % 2) * 128 + 128] = w_fin[matrix, j, i].astype(F32)
        stores[matrix].start()
    for copy in stores:
        copy.wait()


def on_device(dims, features, w_self, w_neigh, adjacency, tile_ids, send_rows, send_counts, hub_rows, cotangent):
    nd, ny, nz, nx = dims
    nodes, width = features.shape
    row_tiles, _, tile, _ = adjacency.shape
    slots, hubs = send_rows.shape[1], hub_rows.shape[1]
    src_tiles = (nodes + nd * slots + nz * nx * hubs) // tile
    crows = nodes // ny // (nx // 2)
    args = (features, w_self, w_neigh, adjacency, tile_ids, send_rows, send_counts, hub_rows, cotangent)
    hbm = pl.BlockSpec(memory_space=pltpu.HBM)
    dma = pltpu.SemaphoreType.DMA
    pairs = [(nd,), (nz,), (nx, 4), (nd,), (nx,), (nz,), (), (ny * nx,), (nz,), (ny * nx,), ()]
    results = pl.pallas_call(
        functools.partial(kernel, dims),
        out_shape=(
            jax.ShapeDtypeStruct((nodes, width), BF16),
            jax.ShapeDtypeStruct((nodes, width), BF16),
            jax.ShapeDtypeStruct((2, nx, ny, crows, 128), BF16),
        ),
        in_specs=[hbm] * len(args),
        out_specs=[hbm] * 3,
        scratch_shapes=[
            (pltpu.SMEM if arg is tile_ids else pltpu.VMEM)(arg.shape, arg.dtype) for arg in args
        ] + [
            dma((len(args),)),
            pltpu.VMEM((nodes, width), BF16),
            pltpu.VMEM((nodes, width), BF16),
            dma((3,)),
            pltpu.VMEM((nd, slots, width), BF16),
            pltpu.VMEM((nd, slots, width), BF16),
            pltpu.VMEM((nx, nz, hubs, width), BF16),
            pltpu.VMEM((src_tiles, nodes, tile), BF16),
            pltpu.VMEM((src_tiles, tile, nodes), BF16),
            pltpu.VMEM((src_tiles, nodes, tile), BF16),
            pltpu.VMEM((src_tiles, tile, nodes), BF16),
            pltpu.VMEM((nd * slots, nodes), BF16),
            pltpu.VMEM((nodes, nd * slots), BF16),
            pltpu.VMEM((2, width, nodes), BF16),
            pltpu.VMEM((nd, slots, width), BF16),
            pltpu.VMEM((nd, slots, width), BF16),
            pltpu.VMEM((nx, nz, hubs, width), BF16),
            pltpu.VMEM((nx, nz, hubs, width), BF16),
            pltpu.VMEM((nz, hubs, width), BF16),
            pltpu.VMEM((nz, hubs, width), BF16),
            pltpu.VMEM((width, width), F32),
            pltpu.VMEM((width, width), F32),
            pltpu.VMEM((ny, nx, crows, 128), BF16),
            pltpu.VMEM((ny * nx, crows, 128), BF16),
            pltpu.VMEM((nz, crows, 128), BF16),
            pltpu.VMEM((2, nx, ny, crows, 128), BF16),
        ] + [dma(shape) for shape in pairs for _ in range(2)],
        compiler_params=pltpu.CompilerParams(
            collective_id=0, has_side_effects=True, vmem_limit_bytes=VMEM_LIMIT),
    )(*args)
    rows = jax.ShapeDtypeStruct((nodes, width), BF16)
    weights = jax.ShapeDtypeStruct((width, width), F32)
    return pl.pallas_call(
        store,
        out_shape=(rows, rows, weights, weights),
        in_specs=[hbm] * 3,
        out_specs=[hbm] * 4,
        scratch_shapes=[pltpu.VMEM(r.shape, r.dtype) for r in (*results, weights, weights)] + [dma((3,)), dma((4,))],
        compiler_params=pltpu.CompilerParams(vmem_limit_bytes=VMEM_LIMIT),
    )(*results)


def solution(mesh):
    nd, ng = mesh.shape["dom"], mesh.shape["grp"]
    dims = (nd, nd // CORES, ng // X_CHIPS, X_CHIPS)
    placed = (
        P(("dom", "grp"), None),
        P(),
        P(),
        P(("dom", "grp"), None, None, None),
        P(("dom", "grp"), None),
        P(("dom", "grp"), None),
        P(("dom", "grp"), None),
        P(("dom", "grp"), None),
        P(("dom", "grp"), None),
    )
    return jax.shard_map(
        functools.partial(on_device, dims),
        mesh=mesh,
        in_specs=placed,
        out_specs=(P(("dom", "grp"), None), P(("dom", "grp"), None), P(), P()),
        check_vma=False,
    )
```

time: 74 us -> 60.2 us (0.81)
  local copies, waits for them, and re-layouts: 10.1 us -> 0 us
  Pallas kernels: 62.9 us -> 59.4 us
    unnamed x22 -> x0, local copies, waits for them, and re-layouts: 10.1 us -> none
    pallas_call x1, Pallas kernels: 62.9 us -> 57.4 us  [on_device(): pl.pallas_call(functools.partial(kernel, dims), out_shape=(jax.ShapeDtype...]
    pallas_call x0 -> x1, Pallas kernels: none -> 1.98 us  [on_device(): pl.pallas_call(store, out_shape=(rows, rows, weights, weights), in_specs=...]
where the time goes in v2:
time: 60.2 us; the launch traced here: 60 us
  Pallas kernels  59.4 us (99%)
  between operations  0.64 us (1%)
    pallas_call x1, Pallas kernels, on_device(): pl.pallas_call(functools.partial(kernel, dims), out_shape=(jax.ShapeDtype...  57.4 us
    pallas_call x1, Pallas kernels, on_device(): pl.pallas_call(store, out_shape=(rows, rows, weights, weights), in_specs=...  1.98 us

profile of v2, /device:TPU:1, one launch (start us, length us, event | category | flops | bytes accessed | tf_op | source)
XLA Modules:
  0.0 60.0 jit_solution(7680713472261056804)
XLA Ops:
  0.6 57.4 %shard_map.120 = (bf16[256,256]{1,0:T(8,128)(2,1)}, bf16[256,256]{1,0:T(8,128)(2,1)}, bf16[2,4,8,16,128]{4,3,2,1,0:T(8,128)(2,1)}) custom-call(bf16[256,256]{1,0:T(8,128)(2,1)} %feat_in.1, bf16[256,256]{1,0:T(8,128)(2,1)} %w_self_in.1, bf16[256,256]{1,0:T(8,128)(2,1)} %w_neigh_in.1, bf16[2,8,128,128]{3,2,1,0:T(8,128)(2,1)} %adj_in.1, s32[2,8]{1,0:T(2,128)} %ids_in.1, ...), custom_call_target="tpu_custom_call" | custom-call | tf_op jit(solution)/shard_map/pallas_call | solution.py:329
  58.1 2.0 %shard_map.121 = (bf16[256,256]{1,0:T(8,128)(2,1)}, bf16[256,256]{1,0:T(8,128)(2,1)}, f32[256,256]{1,0:T(8,128)}, f32[256,256]{1,0:T(8,128)}) custom-call(bf16[256,256]{1,0:T(8,128)(2,1)} %get-tuple-element.7.out_in, bf16[256,256]{1,0:T(8,128)(2,1)} %get-tuple-element.8.grad_in, bf16[2,4,8,16,128]{4,3,2,1,0:T(8,128)(2,1)} %get-tuple-element.9.w_in), custom_call_target="tpu_custom_call" | custom-call | tf_op jit(solution)/shard_map/pallas_call | solution.py:373

commit v3 on v2

--- a/solution.py
+++ b/solution.py
@@ -38,7 +38,7 @@
     out_to, grad_feat_to, w_fin_to,
     feat, w_self, w_neigh, adj, ids, send_rows, send_counts, hub_rows, cot, load_sem,
     out, grad_feat, store_sem,
-    out_send, halo_in, hub_in, dense, dense_t, dense_low, dense_low_t, pick, pick_t, lhs_t,
+    out_send, halo_in, hub_own, hub_in, dense, dense_t, dense_low, dense_low_t, pick, pick_t, lhs_t,
     g_send, g_ret, h_send, h_recv, h2_send, h2_recv,
     gw, w_sib, w2_send, w2_recv, w4_recv, w_fin,
     halo_s, halo_r, hz_s, hz_r, hx_s, hx_r, gh_s, gh_r, gx_s, gx_r, gz_s, gz_r,
@@ -52,7 +52,7 @@
     src_tiles = dense.shape[0]
     own_tiles = nodes // tile
     halo_tiles = nd * slots // tile
-    crows = w_fin.shape[3]
+    crows = w_fin.shape[2]
     me_d = lax.axis_index("dom")
     me_g = lax.axis_index("grp")
     y, core = lax.div(me_d, CORES), lax.rem(me_d, CORES)
@@ -71,20 +71,20 @@
         return lax.rem(y + k, ny)
 
     sibling = y * CORES + (1 - core)
-    pending = []
-
-    def push(src, dst, send_sem, recv_sem, d, g):
-        copy = pltpu.make_async_remote_copy(
+    def copy_of(src, dst, send_sem, recv_sem, d, g):
+        return pltpu.make_async_remote_copy(
             src_ref=src, dst_ref=dst, send_sem=send_sem, recv_sem=recv_sem,
             device_id=(d, g), device_id_type=pl.DeviceIdType.MESH,
         )
-        copy.start()
-        pending.append(copy)
-        return copy
-
-    def arrive(*copies):
-        for copy in copies:
-            copy.wait_recv()
+
+    def push(*copy):
+        copy_of(*copy).start()
+
+    def arrive(size, send_sem, recv_sem):
+        copy_of(size, size, send_sem, recv_sem, sibling, me_g).wait_recv()
+
+    def sent(size, send_sem, recv_sem):
+        copy_of(size, size, send_sem, recv_sem, sibling, me_g).wait_send()
 
     loads = [
         pltpu.make_async_copy(src, dst, load_sem.at[i])
@@ -96,16 +96,16 @@
         load.start()
 
     barrier = pltpu.get_barrier_semaphore()
-    partners = [(dom_at(k), me_g) for k in range(1, nd)]
-    partners += [(me_d, z_at(k) * nx + x) for k in range(1, nz)]
-    partners += [(me_d, z * nx + x_at(k)) for k in range(1, nx)]
+    far_z = [k for (k,) in far_first(nz)]
+    far_x = [k for (k,) in far_first(nx)]
+    far_dom = [i * CORES + j for i, j in far_first(ny, CORES)]
+    partners = [(me_d, z_at(k) * nx + x) for k in far_z]
+    partners += [(me_d, z * nx + x_at(k)) for k in far_x]
+    partners += [(dom_at(k), me_g) for k in far_dom]
     for partner in partners:
         pl.semaphore_signal(barrier, inc=1, device_id=partner, device_id_type=pl.DeviceIdType.MESH)
 
-    far = max(1, nz // 3)
-    far_z = [k for (k,) in far_first(nz)]
-    far_x = [k for (k,) in far_first(nx)]
-    own_slot = nz - far
+    z_group = nz // 4
     for load in loads[:2]:
         load.wait()
     features = feat[...]
@@ -115,22 +115,7 @@
         jnp.where(hub_eye, jnp.broadcast_to(hub_index, (hubs, hubs)), 0.0), axis=1, keepdims=True)
     hub_pick = jnp.where(
         lax.broadcasted_iota(jnp.int32, (hubs, nodes), 1).astype(F32) == hub_col, 1.0, 0.0).astype(BF16)
-    hub_in[x, own_slot] = mm(hub_pick, features).astype(BF16)
-
-    pl.semaphore_wait(barrier, len(partners))
-
-    hub_z = {}
-    for k in far_z:
-        hub_z[k] = push(
-            hub_in.at[x, own_slot], hub_in.at[x, (k - far) % nz], hz_s.at[k], hz_r.at[k], me_d, z_at(k) * nx + x)
-    hub_x = []
-
-    def forward(group, first, last):
-        block = hub_in.at[x, pl.ds(first, last - first)]
-        for j in far_x:
-            hub_x.append(push(block, block, hx_s.at[j, group], hx_r.at[j, group], me_d, z * nx + x_at(j)))
-
-    forward(0, own_slot, own_slot + 1)
+    hub_own[...] = mm(hub_pick, features).astype(BF16)
 
     for load in loads[2:4]:
         load.wait()
@@ -141,17 +126,24 @@
         axis=1, keepdims=True)
     live = lax.broadcasted_iota(jnp.int32, (nd, slots), 1).astype(F32) < count_col
     index = jnp.where(live, send_rows[...].astype(F32), -1.0)
-    eye = lax.broadcasted_iota(jnp.int32, (slots, slots), 0) == lax.broadcasted_iota(jnp.int32, (slots, slots), 1)
-    lane = lax.broadcasted_iota(jnp.int32, (slots, nodes), 1).astype(F32)
-    for p in range(nd):
-        column = jnp.sum(
-            jnp.where(eye, jnp.broadcast_to(index[p:p + 1, :], (slots, slots)), 0.0), axis=1, keepdims=True)
-        pick[p * slots:(p + 1) * slots, :] = jnp.where(lane == column, 1.0, 0.0).astype(BF16)
+    total_slots = nd * slots
+    slot = lax.broadcasted_iota(jnp.int32, (total_slots, slots), 0)
+    own_part = lax.div(lax.broadcasted_iota(jnp.int32, (total_slots, nd), 0), slots) == lax.broadcasted_iota(
+        jnp.int32, (total_slots, nd), 1)
+    spread = mm(jnp.where(own_part, 1.0, 0.0).astype(BF16), index.astype(BF16))
+    spread = jnp.where(lax.rem(slot, slots) == lax.broadcasted_iota(jnp.int32, (total_slots, slots), 1), spread, 0.0)
+    spread = mm(spread.astype(BF16), jnp.ones((slots, nodes), BF16))
+    lane = lax.broadcasted_iota(jnp.int32, (total_slots, nodes), 1).astype(F32)
+    pick[...] = jnp.where(lane == spread, 1.0, 0.0).astype(BF16)
     out_send[...] = mm(pick[...], features).astype(BF16).reshape(nd, slots, width)
     halo_in[me_d] = out_send[me_d]
-    far_dom = [i * CORES + j for i, j in far_first(ny, CORES)]
-    halo = [
-        push(out_send.at[dom_at(k)], halo_in.at[me_d], halo_s.at[k], halo_r.at[k], dom_at(k), me_g) for k in far_dom]
+    pl.semaphore_wait(barrier, len(partners))
+
+    for k in far_z:
+        push(hub_own, hub_in.at[x, z], hz_s, hz_r.at[lax.div(z, z_group)], me_d, z_at(k) * nx + x)
+    pltpu.make_async_copy(hub_own, hub_in.at[x, z], hz_r.at[lax.div(z, z_group)]).start()
+    for k in far_dom:
+        push(out_send.at[dom_at(k)], halo_in.at[me_d], halo_s, halo_r, dom_at(k), me_g)
 
     def gather_tiles(c, carry):
         parts = []
@@ -173,12 +165,11 @@
         load.wait()
     lax.fori_loop(0, src_tiles, gather_tiles, 0)
 
-    arrive(*[hub_z[k] for k in range(far, nz - far + 1)])
-    forward(1, 0, nz - 2 * far + 1)
-    arrive(*[hub_z[k] for k in far_z if not far <= k <= nz - far])
-    if far > 1:
-        forward(2, nz - 2 * far + 1, own_slot)
-        forward(3, own_slot + 1, nz)
+    for group in range(4):
+        block = hub_in.at[x, pl.ds(group * z_group, z_group)]
+        arrive(block, hz_s, hz_r.at[group])
+        for j in far_x:
+            push(block, block, hx_s, hx_r, me_d, z * nx + x_at(j))
 
     sums = []
     for r in range(row_tiles):
@@ -201,11 +192,11 @@
 
     numer = from_tiles(0, own_tiles, features)
     pre = mm(features, w_self[...])
-    arrive(*halo)
+    arrive(halo_in.at[pl.ds(0, nd - 1)], halo_s, halo_r)
     numer = numer + from_tiles(own_tiles, halo_tiles, halo_in[...].reshape(nd * slots, width))
-    arrive(*hub_x)
+    arrive(hub_in.at[pl.ds(0, nx - 1)], hx_s, hx_r)
     hub_rows_all = jnp.concatenate(
-        [hub_in[j, lax.rem(z - i - far + 2 * nz, nz)] for i in range(nz) for j in range(nx)], axis=0)
+        [hub_in[j, i] for i in range(nz) for j in range(nx)], axis=0)
     hub_tiles = src_tiles - own_tiles - halo_tiles
     numer = numer + from_tiles(own_tiles + halo_tiles, hub_tiles, hub_rows_all)
     agg = numer * inverse
@@ -219,59 +210,59 @@
 
     lhs_t[1] = agg_b.astype(F32).T.astype(BF16)
     gw[...] = mm(lhs_t[1 - core], grad_pre)
-    w1 = push(gw, w_sib, w1_s, w1_r, sibling, me_g)
+    push(gw, w_sib, w1_s, w1_r, sibling, me_g)
     mine = mm(lhs_t[core], grad_pre)
 
     grad_num = (mm_nt(grad_pre, w_neigh[...]) * inverse).astype(BF16)
     hub_grad = to_tiles(own_tiles + halo_tiles, hub_tiles, grad_num).astype(BF16)
     for g in range(nz * nx):
         h_send[g % nx, g // nx] = hub_grad[g * hubs:(g + 1) * hubs, :]
+    for j in far_x:
+        push(h_send.at[x_at(j)], h_recv.at[x], gx_s, gx_r, me_d, z * nx + x_at(j))
+    h_recv[x] = h_send[x]
     g_send[...] = to_tiles(own_tiles, halo_tiles, grad_num).astype(BF16).reshape(nd, slots, width)
 
-    arrive(w1)
+    arrive(w_sib, w1_s, w1_r)
     mine = mine + w_sib[...]
     yrows = nodes // ny
     plane = far_first(ny, nx)
     for i in range(ny):
         for j in range(nx):
             top = i * yrows + (j // 2) * crows
-            w2_send[i, j] = mine[top:top + crows, (j % 2) * 128:(j % 2) * 128 + 128].astype(BF16)
-    w2 = [
-        push(w2_send.at[y_at(i), x_at(j)], w2_recv.at[n + 1], w2_s.at[n], w2_r.at[n], y_at(i) * CORES + core,
-             z * nx + x_at(j)) for n, (i, j) in enumerate(plane)]
-    w2_recv[0] = w2_send[y, x]
-    hub_gx = [
-        push(h_send.at[x_at(j)], h_recv.at[x], gx_s.at[j], gx_r.at[j], me_d, z * nx + x_at(j)) for j in far_x]
-    h_recv[x] = h_send[x]
+            w2_send[i * nx + j] = mine[top:top + crows, (j % 2) * 128:(j % 2) * 128 + 128].astype(BF16)
+    for n, (i, j) in enumerate(plane):
+        push(w2_send.at[y_at(i) * nx + x_at(j)], w2_recv.at[n + 1], w2_s, w2_r, y_at(i) * CORES + core,
+             z * nx + x_at(j))
+    w2_recv[0] = w2_send[y * nx + x]
     own_grad = mm_nt(grad_pre, w_self[...]) + to_tiles(0, own_tiles, grad_num)
 
-    arrive(*w2)
+    arrive(w2_recv.at[pl.ds(1, len(plane))], w2_s, w2_r)
     w4_recv[z] = jnp.sum(w2_recv[...].astype(F32), axis=0).astype(BF16)
-    w4 = [
-        push(w4_recv.at[z], w4_recv.at[z], w4_s.at[k], w4_r.at[k], me_d, z_at(k) * nx + x) for k in far_z]
-    ret = [
-        push(g_send.at[dom_at(k)], g_ret.at[me_d], gh_s.at[k], gh_r.at[k], dom_at(k), me_g) for k in far_dom]
+    for k in far_z:
+        push(w4_recv.at[z], w4_recv.at[z], w4_s, w4_r, me_d, z_at(k) * nx + x)
+    for k in far_dom:
+        push(g_send.at[dom_at(k)], g_ret.at[me_d], gh_s, gh_r, dom_at(k), me_g)
     g_ret[me_d] = g_send[me_d]
 
-    arrive(*hub_gx)
+    arrive(h_recv.at[pl.ds(0, nx - 1)], gx_s, gx_r)
     h2_send[...] = jnp.sum(h_recv[...].astype(F32), axis=0).astype(BF16)
 
-    arrive(*w4)
-    w_fin[core, x, y] = jnp.sum(w4_recv[...].astype(F32), axis=0).astype(BF16)
-    w5 = [
-        push(w_fin.at[core, x, y], w_fin.at[core, x, y], w5_s.at[n], w5_r.at[n], y_at(i) * CORES + core,
-             z * nx + x_at(j)) for n, (i, j) in enumerate(plane)]
-    hub_gz = [
-        push(h2_send.at[z_at(k)], h2_recv.at[z], gz_s.at[k], gz_r.at[k], me_d, z_at(k) * nx + x) for k in far_z]
+    arrive(w4_recv.at[pl.ds(0, nz - 1)], w4_s, w4_r)
+    mine_at = w_fin.at[core, x * ny + y]
+    mine_at[...] = jnp.sum(w4_recv[...].astype(F32), axis=0).astype(BF16)
+    for i, j in plane:
+        push(mine_at, mine_at, w5_s, w5_r, y_at(i) * CORES + core, z * nx + x_at(j))
+    for k in far_z:
+        push(h2_send.at[z_at(k)], h2_recv.at[z], gz_s, gz_r, me_d, z_at(k) * nx + x)
     h2_recv[z] = h2_send[z]
 
-    arrive(*ret)
+    arrive(g_ret.at[pl.ds(0, nd - 1)], gh_s, gh_r)
     own_grad = own_grad + mm(pick_t[...], g_ret[...].reshape(nd * slots, width))
 
-    arrive(*w5)
-    w7 = push(w_fin.at[core], w_fin.at[core], w7_s, w7_r, sibling, me_g)
-
-    arrive(*hub_gz)
+    arrive(w_fin.at[core, pl.ds(0, len(plane))], w5_s, w5_r)
+    push(w_fin.at[core], w_fin.at[core], w7_s, w7_r, sibling, me_g)
+
+    arrive(h2_recv.at[pl.ds(0, nz - 1)], gz_s, gz_r)
     hub_total = jnp.sum(h2_recv[...].astype(F32), axis=0)
     hub_pick_t = jnp.where(
         lax.broadcasted_iota(jnp.int32, (nodes, hubs), 0).astype(F32) == jnp.broadcast_to(hub_index, (nodes, hubs)),
@@ -282,16 +273,25 @@
     stores.append(pltpu.make_async_copy(grad_feat, grad_feat_to, store_sem.at[1]))
     stores[-1].start()
 
-    arrive(w7)
+    arrive(w_fin.at[core], w7_s, w7_r)
     stores.append(pltpu.make_async_copy(w_fin, w_fin_to, store_sem.at[2]))
     stores[-1].start()
-    for copy in pending:
-        copy.wait_send()
+    sent(hub_in.at[0, pl.ds(0, nz - 1)], hz_s, hz_r.at[0])
+    sent(hub_in.at[pl.ds(0, nx - 1)], hx_s, hx_r)
+    sent(out_send.at[pl.ds(0, nd - 1)], halo_s, halo_r)
+    sent(gw, w1_s, w1_r)
+    sent(h_send.at[pl.ds(0, nx - 1)], gx_s, gx_r)
+    sent(w2_send.at[pl.ds(0, len(plane))], w2_s, w2_r)
+    sent(w4_recv.at[pl.ds(0, nz - 1)], w4_s, w4_r)
+    sent(g_send.at[pl.ds(0, nd - 1)], gh_s, gh_r)
+    sent(w_fin.at[core, pl.ds(0, len(plane))], w5_s, w5_r)
+    sent(h2_send.at[pl.ds(0, nz - 1)], gz_s, gz_r)
+    sent(w_fin.at[core], w7_s, w7_r)
     for copy in stores:
         copy.wait()
 
 
-def store(out_in, grad_in, w_in, out_to, grad_to, self_to, neigh_to, out, grad, w_fin, grad_self, grad_neigh, load_sem, store_sem):
+def store(ny, out_in, grad_in, w_in, out_to, grad_to, self_to, neigh_to, out, grad, w_fin, grad_self, grad_neigh, load_sem, store_sem):
     loads = [
         pltpu.make_async_copy(src, via, load_sem.at[i])
         for i, (src, via) in enumerate(((w_in, w_fin), (out_in, out), (grad_in, grad)))]
@@ -304,12 +304,13 @@
         load.wait()
     stores[2].start()
     stores[3].start()
-    _, nx, ny, crows, _ = w_fin.shape
+    _, blocks, crows, _ = w_fin.shape
+    nx = blocks // ny
     for matrix, result in enumerate((grad_self, grad_neigh)):
         for j in range(nx):
             for i in range(ny):
                 top = (i * (nx // 2) + j // 2) * crows
-                result[top:top + crows, (j % 2) * 128:(j % 2) * 128 + 128] = w_fin[matrix, j, i].astype(F32)
+                result[top:top + crows, (j % 2) * 128:(j % 2) * 128 + 128] = w_fin[matrix, j * ny + i].astype(F32)
         stores[matrix].start()
     for copy in stores:
         copy.wait()
@@ -325,13 +326,12 @@
     args = (features, w_self, w_neigh, adjacency, tile_ids, send_rows, send_counts, hub_rows, cotangent)
     hbm = pl.BlockSpec(memory_space=pltpu.HBM)
     dma = pltpu.SemaphoreType.DMA
-    pairs = [(nd,), (nz,), (nx, 4), (nd,), (nx,), (nz,), (), (ny * nx,), (nz,), (ny * nx,), ()]
     results = pl.pallas_call(
         functools.partial(kernel, dims),
         out_shape=(
             jax.ShapeDtypeStruct((nodes, width), BF16),
             jax.ShapeDtypeStruct((nodes, width), BF16),
-            jax.ShapeDtypeStruct((2, nx, ny, crows, 128), BF16),
+            jax.ShapeDtypeStruct((2, nx * ny, crows, 128), BF16),
         ),
         in_specs=[hbm] * len(args),
         out_specs=[hbm] * 3,
@@ -344,6 +344,7 @@
             dma((3,)),
             pltpu.VMEM((nd, slots, width), BF16),
             pltpu.VMEM((nd, slots, width), BF16),
+            pltpu.VMEM((hubs, width), BF16),
             pltpu.VMEM((nx, nz, hubs, width), BF16),
             pltpu.VMEM((src_tiles, nodes, tile), BF16),
             pltpu.VMEM((src_tiles, tile, nodes), BF16),
@@ -360,18 +361,18 @@
             pltpu.VMEM((nz, hubs, width), BF16),
             pltpu.VMEM((width, width), F32),
             pltpu.VMEM((width, width), F32),
-            pltpu.VMEM((ny, nx, crows, 128), BF16),
+            pltpu.VMEM((ny * nx, crows, 128), BF16),
             pltpu.VMEM((ny * nx, crows, 128), BF16),
             pltpu.VMEM((nz, crows, 128), BF16),
-            pltpu.VMEM((2, nx, ny, crows, 128), BF16),
-        ] + [dma(shape) for shape in pairs for _ in range(2)],
+            pltpu.VMEM((2, nx * ny, crows, 128), BF16),
+        ] + [dma] * 3 + [dma((4,))] + [dma] * 18,
         compiler_params=pltpu.CompilerParams(
             collective_id=0, has_side_effects=True, vmem_limit_bytes=VMEM_LIMIT),
     )(*args)
     rows = jax.ShapeDtypeStruct((nodes, width), BF16)
     weights = jax.ShapeDtypeStruct((width, width), F32)
     return pl.pallas_call(
-        store,
+        functools.partial(store, ny),
         out_shape=(rows, rows, weights, weights),
         in_specs=[hbm] * 3,
         out_specs=[hbm] * 4,

time: 60.2 us -> 56.7 us (0.942)
  Pallas kernels: 59.4 us -> 55.9 us
    pallas_call x1, Pallas kernels: 57.4 us -> 53.9 us  [on_device(): pl.pallas_call(functools.partial(kernel, dims), out_shape=(jax.ShapeDtype...]
where the time goes in v3:
time: 56.7 us; the launch traced here: 56.6 us
  Pallas kernels  55.9 us (99%)
  between operations  0.64 us (1%)
    pallas_call x1, Pallas kernels, on_device(): pl.pallas_call(functools.partial(kernel, dims), out_shape=(jax.ShapeDtype...  53.9 us
    pallas_call x1, Pallas kernels, on_device(): pl.pallas_call(functools.partial(store, ny), out_shape=(rows, rows, weigh...  1.98 us

profile of v3, /device:TPU:1, one launch (start us, length us, event | category | flops | bytes accessed | tf_op | source)
XLA Modules:
  0.0 56.6 jit_solution(12527593420817700355)
XLA Ops:
  0.6 53.9 %shard_map.120 = (bf16[256,256]{1,0:T(8,128)(2,1)}, bf16[256,256]{1,0:T(8,128)(2,1)}, bf16[2,32,16,128]{3,2,1,0:T(8,128)(2,1)}) custom-call(bf16[256,256]{1,0:T(8,128)(2,1)} %feat_in.1, bf16[256,256]{1,0:T(8,128)(2,1)} %w_self_in.1, bf16[256,256]{1,0:T(8,128)(2,1)} %w_neigh_in.1, bf16[2,8,128,128]{3,2,1,0:T(8,128)(2,1)} %adj_in.1, s32[2,8]{1,0:T(2,128)} %ids_in.1, ...), custom_call_target="tpu_custom_call" | custom-call | tf_op jit(solution)/shard_map/pallas_call | solution.py:329
  54.6 2.0 %shard_map.121 = (bf16[256,256]{1,0:T(8,128)(2,1)}, bf16[256,256]{1,0:T(8,128)(2,1)}, f32[256,256]{1,0:T(8,128)}, f32[256,256]{1,0:T(8,128)}) custom-call(bf16[256,256]{1,0:T(8,128)(2,1)} %get-tuple-element.7.out_in, bf16[256,256]{1,0:T(8,128)(2,1)} %get-tuple-element.8.grad_in, bf16[2,32,16,128]{3,2,1,0:T(8,128)(2,1)} %get-tuple-element.9.w_in), custom_call_target="tpu_custom_call" | custom-call | tf_op jit(solution)/shard_map/pallas_call | solution.py:374

commit v4 on v3

--- a/solution.py
+++ b/solution.py
@@ -105,7 +105,7 @@
     for partner in partners:
         pl.semaphore_signal(barrier, inc=1, device_id=partner, device_id_type=pl.DeviceIdType.MESH)
 
-    z_group = nz // 4
+    z_group = nz // 3
     for load in loads[:2]:
         load.wait()
     features = feat[...]
@@ -165,7 +165,7 @@
         load.wait()
     lax.fori_loop(0, src_tiles, gather_tiles, 0)
 
-    for group in range(4):
+    for group in range(3):
         block = hub_in.at[x, pl.ds(group * z_group, z_group)]
         arrive(block, hz_s, hz_r.at[group])
         for j in far_x:
@@ -300,10 +300,7 @@
         for i, (via, dst) in enumerate(((grad_self, self_to), (grad_neigh, neigh_to), (out, out_to), (grad, grad_to)))]
     for load in loads:
         load.start()
-    for load in loads:
-        load.wait()
-    stores[2].start()
-    stores[3].start()
+    loads[0].wait()
     _, blocks, crows, _ = w_fin.shape
     nx = blocks // ny
     for matrix, result in enumerate((grad_self, grad_neigh)):
@@ -312,6 +309,8 @@
                 top = (i * (nx // 2) + j // 2) * crows
                 result[top:top + crows, (j % 2) * 128:(j % 2) * 128 + 128] = w_fin[matrix, j * ny + i].astype(F32)
         stores[matrix].start()
+        loads[matrix + 1].wait()
+        stores[matrix + 2].start()
     for copy in stores:
         copy.wait()
 
@@ -365,7 +364,7 @@
             pltpu.VMEM((ny * nx, crows, 128), BF16),
             pltpu.VMEM((nz, crows, 128), BF16),
             pltpu.VMEM((2, nx * ny, crows, 128), BF16),
-        ] + [dma] * 3 + [dma((4,))] + [dma] * 18,
+        ] + [dma] * 3 + [dma((3,))] + [dma] * 18,
         compiler_params=pltpu.CompilerParams(
             collective_id=0, has_side_effects=True, vmem_limit_bytes=VMEM_LIMIT),
     )(*args)

time: 56.7 us -> 56.6 us (level)
  no operation moved by 1% of the time
where the time goes in v4:
time: 56.6 us; the launch traced here: 56.4 us
  Pallas kernels  55.8 us (99%)
  between operations  0.64 us (1%)
    pallas_call x1, Pallas kernels, on_device(): pl.pallas_call(functools.partial(kernel, dims), out_shape=(jax.ShapeDtype...  53.9 us
    pallas_call x1, Pallas kernels, on_device(): pl.pallas_call(functools.partial(store, ny), out_shape=(rows, rows, weigh...  1.9 us

profile of v4, /device:TPU:1, one launch (start us, length us, event | category | flops | bytes accessed | tf_op | source)
XLA Modules:
  0.0 56.4 jit_solution(1008128210734677270)
XLA Ops:
  0.6 53.9 %shard_map.120 = (bf16[256,256]{1,0:T(8,128)(2,1)}, bf16[256,256]{1,0:T(8,128)(2,1)}, bf16[2,32,16,128]{3,2,1,0:T(8,128)(2,1)}) custom-call(bf16[256,256]{1,0:T(8,128)(2,1)} %feat_in.1, bf16[256,256]{1,0:T(8,128)(2,1)} %w_self_in.1, bf16[256,256]{1,0:T(8,128)(2,1)} %w_neigh_in.1, bf16[2,8,128,128]{3,2,1,0:T(8,128)(2,1)} %adj_in.1, s32[2,8]{1,0:T(2,128)} %ids_in.1, ...), custom_call_target="tpu_custom_call" | custom-call | tf_op jit(solution)/shard_map/pallas_call | solution.py:328
  54.5 1.9 %shard_map.121 = (bf16[256,256]{1,0:T(8,128)(2,1)}, bf16[256,256]{1,0:T(8,128)(2,1)}, f32[256,256]{1,0:T(8,128)}, f32[256,256]{1,0:T(8,128)}) custom-call(bf16[256,256]{1,0:T(8,128)(2,1)} %get-tuple-element.7.out_in, bf16[256,256]{1,0:T(8,128)(2,1)} %get-tuple-element.8.grad_in, bf16[2,32,16,128]{3,2,1,0:T(8,128)(2,1)} %get-tuple-element.9.w_in), custom_call_target="tpu_custom_call" | custom-call | tf_op jit(solution)/shard_map/pallas_call | solution.py:373

commit v5 on v4

--- a/solution.py
+++ b/solution.py
@@ -261,6 +261,8 @@
 
     arrive(w_fin.at[core, pl.ds(0, len(plane))], w5_s, w5_r)
     push(w_fin.at[core], w_fin.at[core], w7_s, w7_r, sibling, me_g)
+    stores.append(pltpu.make_async_copy(w_fin.at[core], w_fin_to.at[core], store_sem.at[3]))
+    stores[-1].start()
 
     arrive(h2_recv.at[pl.ds(0, nz - 1)], gz_s, gz_r)
     hub_total = jnp.sum(h2_recv[...].astype(F32), axis=0)
@@ -274,7 +276,7 @@
     stores[-1].start()
 
     arrive(w_fin.at[core], w7_s, w7_r)
-    stores.append(pltpu.make_async_copy(w_fin, w_fin_to, store_sem.at[2]))
+    stores.append(pltpu.make_async_copy(w_fin.at[1 - core], w_fin_to.at[1 - core], store_sem.at[2]))
     stores[-1].start()
     sent(hub_in.at[0, pl.ds(0, nz - 1)], hz_s, hz_r.at[0])
     sent(hub_in.at[pl.ds(0, nx - 1)], hx_s, hx_r)
@@ -340,7 +342,7 @@
             dma((len(args),)),
             pltpu.VMEM((nodes, width), BF16),
             pltpu.VMEM((nodes, width), BF16),
-            dma((3,)),
+            dma((4,)),
             pltpu.VMEM((nd, slots, width), BF16),
             pltpu.VMEM((nd, slots, width), BF16),
             pltpu.VMEM((hubs, width), BF16),

time: 56.6 us -> 56.6 us (level)
  no operation moved by 1% of the time
where the time goes in v5:
time: 56.6 us; the launch traced here: 56.4 us
  Pallas kernels  55.7 us (98%)
  between operations  0.64 us (1%)
    pallas_call x1, Pallas kernels, on_device(): pl.pallas_call(functools.partial(kernel, dims), out_shape=(jax.ShapeDtype...  53.8 us
    pallas_call x1, Pallas kernels, on_device(): pl.pallas_call(functools.partial(store, ny), out_shape=(rows, rows, weigh...  1.9 us

profile of v5, /device:TPU:1, one launch (start us, length us, event | category | flops | bytes accessed | tf_op | source)
XLA Modules:
  0.0 56.4 jit_solution(10297739906064805561)
XLA Ops:
  0.6 53.8 %shard_map.120 = (bf16[256,256]{1,0:T(8,128)(2,1)}, bf16[256,256]{1,0:T(8,128)(2,1)}, bf16[2,32,16,128]{3,2,1,0:T(8,128)(2,1)}) custom-call(bf16[256,256]{1,0:T(8,128)(2,1)} %feat_in.1, bf16[256,256]{1,0:T(8,128)(2,1)} %w_self_in.1, bf16[256,256]{1,0:T(8,128)(2,1)} %w_neigh_in.1, bf16[2,8,128,128]{3,2,1,0:T(8,128)(2,1)} %adj_in.1, s32[2,8]{1,0:T(2,128)} %ids_in.1, ...), custom_call_target="tpu_custom_call" | custom-call | tf_op jit(solution)/shard_map/pallas_call | solution.py:330
  54.5 1.9 %shard_map.121 = (bf16[256,256]{1,0:T(8,128)(2,1)}, bf16[256,256]{1,0:T(8,128)(2,1)}, f32[256,256]{1,0:T(8,128)}, f32[256,256]{1,0:T(8,128)}) custom-call(bf16[256,256]{1,0:T(8,128)(2,1)} %get-tuple-element.7.out_in, bf16[256,256]{1,0:T(8,128)(2,1)} %get-tuple-element.8.grad_in, bf16[2,32,16,128]{3,2,1,0:T(8,128)(2,1)} %get-tuple-element.9.w_in), custom_call_target="tpu_custom_call" | custom-call | tf_op jit(solution)/shard_map/pallas_call | solution.py:375
